TPU v7x, 32 devices: a whole 2x2x4 slice. The times are simulated.
32 devices in a mesh: flow: 2 (over x), col: 4 (over y, core), row: 4 (over z).
Axes of the slice: x: 2, y: 2, z: 4, core: 2. Of those that a mesh axis runs over, the one named last changes fastest.
Arguments:
- forcing: float32 [5, 12, 48, 768], P(None, 'flow', 'col', 'row'), may hold values from -6 to 6
- previous: float32 [5, 12, 48, 768], P(None, 'flow', 'col', 'row'), may hold values from -6 to 6
- element_diagonal_shift: float32 [2, 8, 128], P('flow', 'col', 'row'), may hold values from 0.5 to 4
- eigen_bases: float32 [3, 6, 6], replicated, may hold values from -1 to 1, as said below
- eigen_values: float32 [3, 6], replicated, may hold values from 0.5 to 8
- observers: float32 [3, 256], replicated, may hold values from 8 to 30
- panel_points: float32 [3, 1024], P(None, ('flow', 'col', 'row')), may hold values from -2 to 2
- surface_history: float32 [4, 15, 1024], P(None, None, ('flow', 'col', 'row')), may hold values from -6 to 6
Outputs:
- new_state: float32 [5, 12, 48, 768], P(None, 'flow', 'col', 'row')
- spectra: float32 [2, 16, 256], P(None, None, 'row')
Inputs may be any that keep to these rules, and one draw needn't show every extreme that they name: Each eigen_bases[d] is an orthogonal matrix.
All inputs are finite; a program needn't handle non-finite values.
Results may differ from a plain program's by a relative error of at most 0.0003.
Values sent between devices are 32-bit elements; how exact they have to be, the bound alone decides.
A program may use at most 64 MiB of HBM per device.

v0:
```python
import math
import jax
import jax.numpy as jnp
from jax import lax
from jax.sharding import PartitionSpec as P

P_SIZE = 6
SWEEPS = 2
NT = 16
NF = 16
HIGH = lax.Precision.HIGHEST
OMEGA = 0.8
TAU = 0.5
KMAX = 2.0


def with_halo(x, sides, width):
    for axis, dim in sides:
        size, length = (lax.axis_size(axis), x.shape[dim])
        up = [(i, (i + 1) % size) for i in range(size - 1)]
        down = [(j, i) for i, j in up]
        last = lax.slice_in_dim(x, length - width, length, axis=dim)
        first = lax.slice_in_dim(x, 0, width, axis=dim)
        before = lax.ppermute(last, axis, up)
        after = lax.ppermute(first, axis, down)
        x = jnp.concatenate([before, x, after], axis=dim)
    return x


def contract_small(field, matrix, which):
    extent = field.shape
    count = extent[which]
    blocked = field.reshape(extent[:which] + (count // P_SIZE, P_SIZE) + extent[which + 1 :])
    blocked = jnp.moveaxis(blocked, which + 1, -1)
    result = jnp.einsum("...p,qp->...q", blocked, matrix, precision=HIGH)
    result = jnp.moveaxis(result, -1, which + 1)
    return result.reshape(extent)


def contract_last(field, wide_matrix):
    extent = field.shape
    group = wide_matrix.shape[0]
    blocked = field.reshape(extent[0], extent[1], extent[2], extent[3] // group, group)
    result = jnp.einsum("cxybg,hg->cxybh", blocked, wide_matrix, precision=HIGH)
    return result.reshape(extent)


def face_masks(count):
    index = jnp.arange(count) % P_SIZE
    return ((index == P_SIZE - 1).astype(jnp.float32), (index == 0).astype(jnp.float32))


def far_terms(observers, points, source_re, source_im):
    offsets = observers[:, :, None] - points[:, None, :]
    radius = jnp.sqrt(jnp.sum(offsets * offsets, axis=0))
    unit_dir = offsets / radius[None]
    freqs = source_re.shape[1]
    wavenum = (KMAX * (jnp.arange(freqs, dtype=jnp.float32) + 0.5) / freqs)[:, None, None]
    along_re = (
        unit_dir[0][None] * source_re[1][:, None, :]
        + unit_dir[1][None] * source_re[2][:, None, :]
        + unit_dir[2][None] * source_re[3][:, None, :]
    )
    along_im = (
        unit_dir[0][None] * source_im[1][:, None, :]
        + unit_dir[1][None] * source_im[2][:, None, :]
        + unit_dir[2][None] * source_im[3][:, None, :]
    )
    inverse_matrix = 1.0 / radius[None]
    term_re = -wavenum * (source_im[0][:, None, :] + along_im) + along_re * inverse_matrix
    term_im = wavenum * (source_re[0][:, None, :] + along_re) + along_im * inverse_matrix
    phases = wavenum * radius[None]
    amplitude = inverse_matrix / (4.0 * math.pi)
    green_re = amplitude * jnp.cos(phases)
    green_im = -amplitude * jnp.sin(phases)
    total_re = jnp.sum(green_re * term_re - green_im * term_im, axis=2)
    total_im = jnp.sum(green_re * term_im + green_im * term_re, axis=2)
    return jnp.stack([total_re, total_im])


def transform(samples):
    times = jnp.arange(NT, dtype=jnp.float32)
    omegas = math.pi * (jnp.arange(NF, dtype=jnp.float32) + 0.5) / NF
    cos_table = jnp.cos(omegas[:, None] * times[None, :])
    sin_table = jnp.sin(omegas[:, None] * times[None, :])
    source_re = jnp.einsum("fn,cnp->cfp", cos_table, samples, precision=HIGH)
    source_im = -jnp.einsum("fn,cnp->cfp", sin_table, samples, precision=HIGH)
    return (source_re, source_im)


def on_device(
    forcing,
    previous,
    element_diagonal_shift,
    eigen_bases,
    eigen_values,
    observers,
    panel_points,
    surface_history,
):
    extent = forcing.shape
    stiffness = [
        jnp.dot(
            eigen_bases[axis_num] * eigen_values[axis_num][None, :],
            eigen_bases[axis_num].T,
            precision=HIGH,
        )
        for axis_num in range(3)
    ]
    group = P_SIZE * math.gcd(extent[3] // P_SIZE, 64)
    identity = jnp.eye(group // P_SIZE, dtype=jnp.float32)
    wide_stiff = jnp.kron(identity, stiffness[2])
    wide_forward = jnp.kron(identity, eigen_bases[2].T)
    wide_back = jnp.kron(identity, eigen_bases[2])
    shift_nodes = jnp.repeat(
        jnp.repeat(jnp.repeat(element_diagonal_shift, P_SIZE, 0), P_SIZE, 1), P_SIZE, 2
    )
    denominator = (
        shift_nodes
        + jnp.tile(eigen_values[0], extent[1] // P_SIZE)[:, None, None]
        + jnp.tile(eigen_values[1], extent[2] // P_SIZE)[None, :, None]
        + jnp.tile(eigen_values[2], extent[3] // P_SIZE)[None, None, :]
    )
    high_x, low_x = face_masks(extent[1])
    high_y, low_y = face_masks(extent[2])
    high_z, low_z = face_masks(extent[3])
    state = previous
    for sweep in range(SWEEPS):
        apply_result = shift_nodes[None] * state + contract_small(state, stiffness[0], 1)
        apply_result = apply_result + contract_small(state, stiffness[1], 2)
        padded = with_halo(state, (("flow", 1), ("col", 2), ("row", 3)), 1)
        next_x = padded[:, 2:, 1:-1, 1:-1]
        prev_x = padded[:, :-2, 1:-1, 1:-1]
        next_y = padded[:, 1:-1, 2:, 1:-1]
        prev_y = padded[:, 1:-1, :-2, 1:-1]
        next_z = padded[:, 1:-1, 1:-1, 2:]
        prev_z = padded[:, 1:-1, 1:-1, :-2]
        result = high_x[None, :, None, None] * next_x + low_x[None, :, None, None] * prev_x
        result = result + high_y[None, None, :, None] * next_y + low_y[None, None, :, None] * prev_y
        residual = (
            forcing
            - (apply_result + contract_last(state, wide_stiff))
            + TAU
            * (result + high_z[None, None, None, :] * next_z + low_z[None, None, None, :] * prev_z)
        )
        block_result = contract_small(residual, eigen_bases[0].T, 1)
        block_result = contract_small(block_result, eigen_bases[1].T, 2)
        block_result = contract_last(block_result, wide_forward) / denominator[None]
        block_result = contract_small(block_result, eigen_bases[0], 1)
        block_result = contract_small(block_result, eigen_bases[1], 2)
        state = state + OMEGA * contract_last(block_result, wide_back)
    own_panels = panel_points.shape[1]
    newest = state[:4, 0, 0, :own_panels]
    surface_samples = jnp.concatenate([surface_history, newest[:, None, :]], axis=1)
    rows = lax.axis_size("row")
    count = observers.shape[1] // rows
    points, samples = (
        lax.all_gather(panel_points, "row", axis=1, tiled=True),
        lax.all_gather(surface_samples, "row", axis=2, tiled=True),
    )
    source_re, source_im = transform(samples)
    own_obs = lax.dynamic_slice_in_dim(observers, lax.axis_index("row") * count, count, 1)
    partial_sums = far_terms(own_obs, points, source_re, source_im)
    spectra = lax.psum(partial_sums, ("flow", "col"))
    return (state, spectra)


def solution(mesh):
    return jax.shard_map(
        on_device,
        mesh=mesh,
        in_specs=(
            P(None, "flow", "col", "row"),
            P(None, "flow", "col", "row"),
            P("flow", "col", "row"),
            P(),
            P(),
            P(),
            P(None, ("flow", "col", "row")),
            P(None, None, ("flow", "col", "row")),
        ),
        out_specs=(P(None, "flow", "col", "row"), P(None, None, "row")),
        check_vma=False,
    )
```

profile of v0, /device:TPU:0, one launch (start us, length us, event | category | flops | bytes accessed | tf_op | source)
XLA Modules:
  0.0 143.8 jit_solution(3606890502460777156)
XLA Ops:
  0.6 0.9 fusion.168
  1.7 1.3 collective-permute-start
  3.0 4.8 %collective-permute-start.1 = (f32[5,1,12,192]{3,1,2,0:T(1,128)S(1)}, f32[5,1,12,192]{3,1,2,0:T(1,128)S(1)}, u32[]{:S(2)}, u32[]{:S(2)}) collective-permute-start(f32[5,1,12,192]{3,1,2,0:T(1,128)S(1)} %copy.139), channel_id=1, source_target_pairs={{0,16},{1,17},{2,18},{3,19},{4,20},{5,21},{6,22},{7,23},{8,24},{9,... | collective-permute-start | bytes 138248 | tf_op jit(solution)/shard_map/ppermute | solution.py:24
  7.9 1.3 copy.153
  9.2 0.7 slice_bitcast_fusion.12
  10.0 0.8 slice_bitcast_fusion.15
  10.8 0.9 fusion.131
  11.7 4.9 %broadcast_multiply_fusion = (f32[32,6,32,6]{3,2,1,0:T(8,128)}, f32[32,6,32,6]{3,2,1,0:T(8,128)}, f32[32,6,32,6]{3,2,1,0:T(8,128)}) fusion(f32[6,6]{1,0:T(8,128)S(1)} %get-tuple-element.42, f32[32,32]{1,0:T(8,128)S(1)} %fusion.118, f32[6,6]{1,0:T(8,128)S(1)} %copy.146, f32[6,6]{1,0:T(8,128)S(1)} %fusion.131), kind=kLoop, calls=%fused_computation | loop fusion | flops 110592 | bytes 446896 | tf_op jit(solution)/shard_map/jit(kron)/mul | solution.py:114
  16.6 3.9 %reshape.301 = f32[192,192,1,1]{1,0,2,3:T(8,128)S(1)} reshape(f32[32,6,32,6]{3,2,1,0:T(8,128)} %get-tuple-element.41) | data formatting | bytes 294912 | tf_op jit(solution)/shard_map/jit(kron)/mul | solution.py:112
  20.6 0.7 convolution_bitcast_fusion.6
  22.9 13.2 %all-gather = f32[4,32,3]{1,2,0:T(4,128)S(1)} all-gather(f32[1,32,3]{1,2,0:T(4,128)S(1)} %bitcast.282), channel_id=1, replica_groups=mesh['flow'=2,'col'=4,'row'=4] {'row'}, dimensions={0}, use_global_device_ids=true | all-gather | bytes 1920 | tf_op jit(solution)/shard_map/all_gather | solution.py:158
  36.4 0.7 broadcast_multiply_fusion.3
  37.2 0.6 slice_bitcast_fusion.2
  37.8 0.7 add_add_fusion
  38.5 1.1 fusion.3
  39.7 1.3 collective-permute-start.2
  41.0 3.0 %collective-permute-start.3 = (f32[5,8,1,192]{3,1,2,0:T(8,128)S(1)}, f32[5,8,1,192]{3,1,2,0:T(8,128)S(1)}, u32[]{:S(2)}, u32[]{:S(2)}) collective-permute-start(f32[5,8,1,192]{3,1,2,0:T(8,128)S(1)} %get-tuple-element.14), channel_id=1, source_target_pairs={{0,4},{4,8},{8,12},{1,5},{5,9},{9,13},{2,6},{6,10},{10,14},{3,7},{... | collective-permute-start | bytes 92168 | tf_op jit(solution)/shard_map/ppermute | solution.py:24
  44.1 0.8 collective-permute-done.3
  45.3 4.2 %collective-permute-start.5 = (f32[5,8,14,1]{3,1,2,0:T(8,128)S(1)}, f32[5,8,14,1]{3,1,2,0:T(8,128)}, u32[]{:S(2)}, u32[]{:S(2)}) collective-permute-start(f32[5,8,14,1]{3,1,2,0:T(8,128)S(1)} %get-tuple-element.19), channel_id=1, source_target_pairs={{0,1},{1,2},{2,3},{4,5},{5,6},{6,7},{8,9},{9,10},{10,11},{12,13},{... | collective-permute-start | bytes 6728 | tf_op jit(solution)/shard_map/ppermute | solution.py:24
  49.5 1.5 %collective-permute-start.4 = (f32[5,8,14,1]{3,1,2,0:T(8,128)S(1)}, f32[5,8,14,1]{3,1,2,0:T(8,128)}, u32[]{:S(2)}, u32[]{:S(2)}) collective-permute-start(f32[5,8,14,1]{3,1,2,0:T(8,128)S(1)} %get-tuple-element.18), channel_id=1, source_target_pairs={{1,0},{2,1},{3,2},{5,4},{6,5},{7,6},{9,8},{10,9},{11,10},{13,12},{... | collective-permute-start | bytes 6728 | tf_op jit(solution)/shard_map/ppermute | solution.py:25
  51.0 3.9 %reshape.304 = f32[192,192,1,1]{1,0,2,3:T(8,128)S(1)} reshape(f32[32,6,32,6]{3,2,1,0:T(8,128)} %get-tuple-element.40) | data formatting | bytes 294912 | tf_op jit(solution)/shard_map/jit(kron)/mul | solution.py:113
  54.8 3.9 %reshape.307 = f32[192,192,1,1]{1,0,2,3:T(8,128)S(1)} reshape(f32[32,6,32,6]{3,2,1,0:T(8,128)} %get-tuple-element.39) | data formatting | bytes 294912 | tf_op jit(solution)/shard_map/jit(kron)/mul | solution.py:114
  58.8 2.2 %collective-permute-done.4 = f32[5,8,14,1]{3,1,2,0:T(8,128)} collective-permute-done((f32[5,8,14,1]{3,1,2,0:T(8,128)S(1)}, f32[5,8,14,1]{3,1,2,0:T(8,128)}, u32[]{:S(2)}, u32[]{:S(2)}) %collective-permute-start.4) | collective-permute-done | bytes 2272 | tf_op jit(solution)/shard_map/ppermute | solution.py:25
  61.0 2.7 %fusion.55 = f32[5,12,192,6]{2,3,1,0:T(8,128)S(1)} fusion(f32[5,6,12,192]{3,1,2,0:T(8,128)S(1)} %fusion.3, f32[5,8,14,1]{3,1,2,0:T(8,128)} %collective-permute-done.5, f32[5,8,1,192]{3,1,2,0:T(8,128)S(1)} %collective-permute-done.2, f32[5,8,1,192]{3,1,2,0:T(8,128)S(1)} %collective-permute-done.3, f32[5,1,12,192]{3,1,2,0:T(1,128)S(1)} %collective-permute-done, ...), kind=kOutput, calls=%fused_computation.96 | convolution fusion | flops 7119360 | bytes 1476992 | tf_op jit(solution)/shard_map/...p,qp->...q/dot_general | solution.py:35
  63.8 0.6 convolution_bitcast_fusion.5
  65.3 0.8 fusion.90
  66.1 0.6 convolution_bitcast_fusion.4
  66.9 0.8 fusion.10
  67.9 1.3 collective-permute-start.6
  69.2 4.5 %collective-permute-start.7 = (f32[5,1,12,192]{3,1,2,0:T(1,128)S(1)}, f32[5,1,12,192]{3,1,2,0:T(1,128)S(1)}, u32[]{:S(2)}, u32[]{:S(2)}) collective-permute-start(f32[5,1,12,192]{3,1,2,0:T(1,128)S(1)} %get-tuple-element.20), channel_id=1, source_target_pairs={{0,16},{1,17},{2,18},{3,19},{4,20},{5,21},{6,22},{7,23},{8,24},{9,... | collective-permute-start | bytes 138248 | tf_op jit(solution)/shard_map/ppermute | solution.py:24
  74.4 1.2 collective-permute-done.7
  75.6 1.3 collective-permute-start.8
  76.9 3.3 %collective-permute-start.9 = (f32[5,8,1,192]{3,1,2,0:T(8,128)S(1)}, f32[5,8,1,192]{3,1,2,0:T(8,128)S(1)}, u32[]{:S(2)}, u32[]{:S(2)}) collective-permute-start(f32[5,8,1,192]{3,1,2,0:T(8,128)S(1)} %get-tuple-element.12), channel_id=1, source_target_pairs={{0,4},{4,8},{8,12},{1,5},{5,9},{9,13},{2,6},{6,10},{10,14},{3,7},{... | collective-permute-start | bytes 92168 | tf_op jit(solution)/shard_map/ppermute | solution.py:24
  80.2 0.6 convolution_bitcast_fusion.2
  81.4 2.4 %collective-permute-start.11 = (f32[5,8,14,1]{3,1,2,0:T(8,128)S(1)}, f32[5,8,14,1]{3,1,2,0:T(8,128)S(1)}, u32[]{:S(2)}, u32[]{:S(2)}) collective-permute-start(f32[5,8,14,1]{3,1,2,0:T(8,128)S(1)} %get-tuple-element.17), channel_id=1, source_target_pairs={{0,1},{1,2},{2,3},{4,5},{5,6},{6,7},{8,9},{9,10},{10,11},{12,13},{... | collective-permute-start | bytes 6728 | tf_op jit(solution)/shard_map/ppermute | solution.py:24
  83.8 1.3 collective-permute-start.10
  85.1 0.8 fusion.7
  85.9 2.9 %collective-permute-done.11 = f32[5,8,14,1]{3,1,2,0:T(8,128)S(1)} collective-permute-done((f32[5,8,14,1]{3,1,2,0:T(8,128)S(1)}, f32[5,8,14,1]{3,1,2,0:T(8,128)S(1)}, u32[]{:S(2)}, u32[]{:S(2)}) %collective-permute-start.11) | collective-permute-done | bytes 2272 | tf_op jit(solution)/shard_map/ppermute | solution.py:24
  88.8 4.7 %collective-permute-done.10 = f32[5,8,14,1]{3,1,2,0:T(8,128)S(1)} collective-permute-done((f32[5,8,14,1]{3,1,2,0:T(8,128)S(1)}, f32[5,8,14,1]{3,1,2,0:T(8,128)S(1)}, u32[]{:S(2)}, u32[]{:S(2)}) %collective-permute-start.10) | collective-permute-done | bytes 2272 | tf_op jit(solution)/shard_map/ppermute | solution.py:25
  93.5 1.7 %fusion.28 = f32[5,12,192,6]{2,3,1,0:T(8,128)S(1)} fusion(f32[5,6,12,192]{3,1,2,0:T(8,128)S(1)} %fusion.7, f32[5,8,14,1]{3,1,2,0:T(8,128)S(1)} %collective-permute-done.11, f32[5,8,1,192]{3,1,2,0:T(8,128)S(1)} %collective-permute-done.8, f32[5,8,1,192]{3,1,2,0:T(8,128)S(1)} %collective-permute-done.9, f32[5,1,12,192]{3,1,2,0:T(1,128)S(1)} %collective-permute-done.6, ...), kind=kOutput, calls=%fused_computation.57 | convolution fusion | flops 7119360 | bytes 2045952 | tf_op jit(solution)/shard_map/...p,qp->...q/dot_general | solution.py:35
  95.2 0.6 convolution_bitcast_fusion.1
  96.7 0.8 fusion.84
  97.5 0.6 convolution_bitcast_fusion
  98.3 0.7 fusion.8
  99.0 0.9 copy.174
  100.2 14.4 %all_gather.7 = f32[4,16,128]{1,0,2:T(4,128)S(1)} all-gather(f32[4,16,32]{1,0,2:T(4,128)S(1)} %pad_maximum_fusion.62), channel_id=1, replica_groups=mesh['flow'=2,'col'=4,'row'=4] {'row'}, dimensions={2}, use_global_device_ids=true | all-gather | bytes 40960 | tf_op jit(solution)/shard_map/all_gather | solution.py:159
  115.4 2.7 %fusion.17 = (f32[16,64]{1,0:T(8,128)S(1)}, f32[16,64]{1,0:T(8,128)S(1)}) fusion(f32[16,128]{1,0:T(8,128)S(1)} %get-tuple-element.36, f32[64,128]{1,0:T(8,128)S(1)} %copy-done.6, f32[64,128]{1,0:T(8,128)S(1)} %copy-done.7, f32[16,128]{1,0:T(8,128)S(1)} %get-tuple-element.37, f32[16,128]{1,0:T(8,128)S(1)} %get-tuple-element.38, ...), kind=kLoop, calls=%fused_computation.41 | loop fusion | flops 3799040 | bytes 303232 | tf_op jit(solution)/shard_map/reduce_sum | solution.py:76
  118.1 25.7 %psum.7 = f32[2,16,64]{2,1,0:T(8,128)} all-reduce(f32[2,16,64]{2,1,0:T(8,128)S(1)} %pad_maximum_fusion.69), channel_id=1, replica_groups=mesh['flow'=2,'col'=4,'row'=4] {'flow','col'}, use_global_device_ids=true, to_apply=%region_3.4 | all-reduce | flops 2048 | bytes 16384 | tf_op jit(solution)/shard_map/psum | solution.py:164
  (86 shorter events, 7.0 us)
Async XLA Ops:
  0.6 35.6 %copy-start = (f32[3,256]{1,0:T(4,128)S(1)}, f32[3,256]{1,0:T(4,128)}, u32[]{:S(2)}) copy-start(f32[3,256]{1,0:T(4,128)} %param.13) | copy-start | bytes 9220
  1.7 38.0 %collective-permute-start = (f32[5,1,12,192]{3,1,2,0:T(1,128)S(1)}, f32[5,1,12,192]{3,1,2,0:T(1,128)S(1)}, u32[]{:S(2)}, u32[]{:S(2)}) collective-permute-start(f32[5,1,12,192]{3,1,2,0:T(1,128)S(1)} %copy.137), channel_id=1, source_target_pairs={{16,0},{17,1},{18,2},{19,3},{20,4},{21,5},{22,6},{23,7},{24,8},{25... | collective-permute-start | bytes 138248 | tf_op jit(solution)/shard_map/ppermute | solution.py:25
  3.0 36.6 %collective-permute-start.1 = (f32[5,1,12,192]{3,1,2,0:T(1,128)S(1)}, f32[5,1,12,192]{3,1,2,0:T(1,128)S(1)}, u32[]{:S(2)}, u32[]{:S(2)}) collective-permute-start(f32[5,1,12,192]{3,1,2,0:T(1,128)S(1)} %copy.139), channel_id=1, source_target_pairs={{0,16},{1,17},{2,18},{3,19},{4,20},{5,21},{6,22},{7,23},{8,24},{9,... | collective-permute-start | bytes 138248 | tf_op jit(solution)/shard_map/ppermute | solution.py:24
  16.6 4.0 %copy-start.1 = (f32[5,6,12,192]{3,2,1,0:T(8,128)S(1)}, f32[5,6,12,192]{3,2,1,0:T(8,128)}, u32[]{:S(2)}) copy-start(f32[5,6,12,192]{3,2,1,0:T(8,128)} %param.9) | copy-start | bytes 829444
  16.6 4.7 %copy-start.3 = (f32[3,6,6]{2,1,0:T(8,128)S(1)}, f32[3,6,6]{2,1,0:T(8,128)}, u32[]{:S(2)}) copy-start(f32[3,6,6]{2,1,0:T(8,128)} %param.11) | copy-start | bytes 1300
  16.6 5.8 %copy-start.13 = (f32[1,2,32]{2,1,0:T(2,128)S(1)}, f32[1,2,32]{2,1,0:T(2,128)}, u32[]{:S(2)}) copy-start(f32[1,2,32]{2,1,0:T(2,128)} %param.10) | copy-start | bytes 772
  16.6 6.3 %copy-start.12 = (f32[3,32]{1,0:T(4,128)S(1)}, f32[3,32]{1,0:T(4,128)}, u32[]{:S(2)}) copy-start(f32[3,32]{1,0:T(4,128)} %param.14) | copy-start | bytes 1156
  16.6 21.9 %copy-start.2 = (f32[5,6,12,192]{3,2,1,0:T(8,128)S(1)}, f32[5,6,12,192]{3,2,1,0:T(8,128)}, u32[]{:S(2)}) copy-start(f32[5,6,12,192]{3,2,1,0:T(8,128)} %param.8) | copy-start | bytes 829444
  39.7 4.4 %collective-permute-start.2 = (f32[5,8,1,192]{3,1,2,0:T(8,128)S(1)}, f32[5,8,1,192]{3,1,2,0:T(8,128)S(1)}, u32[]{:S(2)}, u32[]{:S(2)}) collective-permute-start(f32[5,8,1,192]{3,1,2,0:T(8,128)S(1)} %get-tuple-element.15), channel_id=1, source_target_pairs={{4,0},{8,4},{12,8},{5,1},{9,5},{13,9},{6,2},{10,6},{14,10},{7,3},{... | collective-permute-start | bytes 92168 | tf_op jit(solution)/shard_map/ppermute | solution.py:25
  41.0 3.9 %collective-permute-start.3 = (f32[5,8,1,192]{3,1,2,0:T(8,128)S(1)}, f32[5,8,1,192]{3,1,2,0:T(8,128)S(1)}, u32[]{:S(2)}, u32[]{:S(2)}) collective-permute-start(f32[5,8,1,192]{3,1,2,0:T(8,128)S(1)} %get-tuple-element.14), channel_id=1, source_target_pairs={{0,4},{4,8},{8,12},{1,5},{5,9},{9,13},{2,6},{6,10},{10,14},{3,7},{... | collective-permute-start | bytes 92168 | tf_op jit(solution)/shard_map/ppermute | solution.py:24
  45.3 13.6 %collective-permute-start.5 = (f32[5,8,14,1]{3,1,2,0:T(8,128)S(1)}, f32[5,8,14,1]{3,1,2,0:T(8,128)}, u32[]{:S(2)}, u32[]{:S(2)}) collective-permute-start(f32[5,8,14,1]{3,1,2,0:T(8,128)S(1)} %get-tuple-element.19), channel_id=1, source_target_pairs={{0,1},{1,2},{2,3},{4,5},{5,6},{6,7},{8,9},{9,10},{10,11},{12,13},{... | collective-permute-start | bytes 6728 | tf_op jit(solution)/shard_map/ppermute | solution.py:24
  49.5 11.6 %collective-permute-start.4 = (f32[5,8,14,1]{3,1,2,0:T(8,128)S(1)}, f32[5,8,14,1]{3,1,2,0:T(8,128)}, u32[]{:S(2)}, u32[]{:S(2)}) collective-permute-start(f32[5,8,14,1]{3,1,2,0:T(8,128)S(1)} %get-tuple-element.18), channel_id=1, source_target_pairs={{1,0},{2,1},{3,2},{5,4},{6,5},{7,6},{9,8},{10,9},{11,10},{13,12},{... | collective-permute-start | bytes 6728 | tf_op jit(solution)/shard_map/ppermute | solution.py:25
  51.0 7.7 %copy-start.11 = (f32[4,15,32]{2,0,1:T(4,128)S(1)}, f32[4,15,32]{2,0,1:T(4,128)}, u32[]{:S(2)}) copy-start(f32[4,15,32]{2,0,1:T(4,128)} %param.15) | copy-start | bytes 23044
  61.0 3.6 %copy-start.4 = (f32[6,12,192]{2,1,0:T(8,128)S(1)}, f32[6,12,192]{2,1,0:T(8,128)}, u32[]{:S(2)}) copy-start(f32[6,12,192]{2,1,0:T(8,128)} %add_add_fusion) | copy-start | bytes 165892
  67.9 6.5 %collective-permute-start.6 = (f32[5,1,12,192]{3,1,2,0:T(1,128)S(1)}, f32[5,1,12,192]{3,1,2,0:T(1,128)S(1)}, u32[]{:S(2)}, u32[]{:S(2)}) collective-permute-start(f32[5,1,12,192]{3,1,2,0:T(1,128)S(1)} %get-tuple-element.21), channel_id=1, source_target_pairs={{16,0},{17,1},{18,2},{19,3},{20,4},{21,5},{22,6},{23,7},{24,8},{25... | collective-permute-start | bytes 138248 | tf_op jit(solution)/shard_map/ppermute | solution.py:25
  69.2 6.4 %collective-permute-start.7 = (f32[5,1,12,192]{3,1,2,0:T(1,128)S(1)}, f32[5,1,12,192]{3,1,2,0:T(1,128)S(1)}, u32[]{:S(2)}, u32[]{:S(2)}) collective-permute-start(f32[5,1,12,192]{3,1,2,0:T(1,128)S(1)} %get-tuple-element.20), channel_id=1, source_target_pairs={{0,16},{1,17},{2,18},{3,19},{4,20},{5,21},{6,22},{7,23},{8,24},{9,... | collective-permute-start | bytes 138248 | tf_op jit(solution)/shard_map/ppermute | solution.py:24
  75.6 5.4 %collective-permute-start.8 = (f32[5,8,1,192]{3,1,2,0:T(8,128)S(1)}, f32[5,8,1,192]{3,1,2,0:T(8,128)S(1)}, u32[]{:S(2)}, u32[]{:S(2)}) collective-permute-start(f32[5,8,1,192]{3,1,2,0:T(8,128)S(1)} %get-tuple-element.13), channel_id=1, source_target_pairs={{4,0},{8,4},{12,8},{5,1},{9,5},{13,9},{6,2},{10,6},{14,10},{7,3},{... | collective-permute-start | bytes 92168 | tf_op jit(solution)/shard_map/ppermute | solution.py:25
  76.9 4.1 %collective-permute-start.9 = (f32[5,8,1,192]{3,1,2,0:T(8,128)S(1)}, f32[5,8,1,192]{3,1,2,0:T(8,128)S(1)}, u32[]{:S(2)}, u32[]{:S(2)}) collective-permute-start(f32[5,8,1,192]{3,1,2,0:T(8,128)S(1)} %get-tuple-element.12), channel_id=1, source_target_pairs={{0,4},{4,8},{8,12},{1,5},{5,9},{9,13},{2,6},{6,10},{10,14},{3,7},{... | collective-permute-start | bytes 92168 | tf_op jit(solution)/shard_map/ppermute | solution.py:24
  81.4 7.4 %collective-permute-start.11 = (f32[5,8,14,1]{3,1,2,0:T(8,128)S(1)}, f32[5,8,14,1]{3,1,2,0:T(8,128)S(1)}, u32[]{:S(2)}, u32[]{:S(2)}) collective-permute-start(f32[5,8,14,1]{3,1,2,0:T(8,128)S(1)} %get-tuple-element.17), channel_id=1, source_target_pairs={{0,1},{1,2},{2,3},{4,5},{5,6},{6,7},{8,9},{9,10},{10,11},{12,13},{... | collective-permute-start | bytes 6728 | tf_op jit(solution)/shard_map/ppermute | solution.py:24
  83.8 9.7 %collective-permute-start.10 = (f32[5,8,14,1]{3,1,2,0:T(8,128)S(1)}, f32[5,8,14,1]{3,1,2,0:T(8,128)S(1)}, u32[]{:S(2)}, u32[]{:S(2)}) collective-permute-start(f32[5,8,14,1]{3,1,2,0:T(8,128)S(1)} %get-tuple-element.16), channel_id=1, source_target_pairs={{1,0},{2,1},{3,2},{5,4},{6,5},{7,6},{9,8},{10,9},{11,10},{13,12},{... | collective-permute-start | bytes 6728 | tf_op jit(solution)/shard_map/ppermute | solution.py:25
  97.4 17.9 %copy-start.5 = (f32[64,128]{1,0:T(8,128)S(1)}, f32[64,128]{1,0:T(8,128)}, u32[]{:S(2)}) copy-start(f32[64,128]{1,0:T(8,128)} %get-tuple-element.27) | copy-start | bytes 98308
  97.4 17.9 %copy-start.6 = (f32[64,128]{1,0:T(8,128)S(1)}, f32[64,128]{1,0:T(8,128)}, u32[]{:S(2)}) copy-start(f32[64,128]{1,0:T(8,128)} %get-tuple-element.28) | copy-start | bytes 98308
  97.4 17.9 %copy-start.7 = (f32[64,128]{1,0:T(8,128)S(1)}, f32[64,128]{1,0:T(8,128)}, u32[]{:S(2)}) copy-start(f32[64,128]{1,0:T(8,128)} %get-tuple-element.30) | copy-start | bytes 98308
  97.4 17.9 %copy-start.8 = (f32[64,128]{1,0:T(8,128)S(1)}, f32[64,128]{1,0:T(8,128)}, u32[]{:S(2)}) copy-start(f32[64,128]{1,0:T(8,128)} %get-tuple-element.24) | copy-start | bytes 98308
  97.5 17.9 %copy-start.9 = (f32[64,128]{1,0:T(8,128)S(1)}, f32[64,128]{1,0:T(8,128)}, u32[]{:S(2)}) copy-start(f32[64,128]{1,0:T(8,128)} %get-tuple-element.25) | copy-start | bytes 98308
  97.5 17.9 %copy-start.10 = (f32[64,128]{1,0:T(8,128)S(1)}, f32[64,128]{1,0:T(8,128)}, u32[]{:S(2)}) copy-start(f32[64,128]{1,0:T(8,128)} %get-tuple-element.26) | copy-start | bytes 98308
where the time goes:
time: 144 us
  blocking collectives  53.4 us (37%)
  starting transfers between devices  30.3 us (21%)
  local copies, waits for them, and re-layouts  19.8 us (14%)
  matrix products  17.4 us (12%)
  waiting for transfers between devices  11.9 us (8%)
  other arithmetic  9.8 us (7%)
    psum x1, blocking collectives, on_device(): spectra = lax.psum(partial_sums, ('flow', 'col'))  25.7 us
    ppermute x6, starting transfers between devices, with_halo(): before = lax.ppermute(last, axis, up)  22.3 us
    all_gather x1, blocking collectives, on_device(): lax.all_gather(surface_samples, 'row', axis=2, tiled=True)  14.4 us
    all_gather x1, blocking collectives, on_device(): lax.all_gather(panel_points, 'row', axis=1, tiled=True)  13.2 us
    dot_general x12, matrix products, contract_small(): result = jnp.einsum('...p,qp->...q', blocked, matrix, precision=HIGH)  11.6 us
    ppermute x6, starting transfers between devices, with_halo(): after = lax.ppermute(first, axis, down)  7.92 us
    ppermute x6, waiting for transfers between devices, with_halo(): after = lax.ppermute(first, axis, down)  6.94 us
    mul x1, other arithmetic, on_device(): wide_back = jnp.kron(identity, eigen_bases[2])  4.95 us
  transfers between devices with their start and end apart: 12, of which 5 were waited for; matrix products, arithmetic and copies ran while one was open for 20% of the time, Pallas kernels for 0%

commit v1 on v0

--- a/solution.py
+++ b/solution.py
@@ -1,3 +1,4 @@
+import functools
 import math
 import jax
 import jax.numpy as jnp
@@ -12,6 +13,13 @@
 OMEGA = 0.8
 TAU = 0.5
 KMAX = 2.0
+
+
+def switch_ladders_here(mat, mesh_ax):
+    return jax.lax.all_gather(mat, mesh_ax).sum(axis=0)
+
+
+choose_tails = functools.partial(switch_ladders_here, mesh_ax=("flow", "col"))
 
 
 def with_halo(x, sides, width):
@@ -161,7 +169,7 @@
     source_re, source_im = transform(samples)
     own_obs = lax.dynamic_slice_in_dim(observers, lax.axis_index("row") * count, count, 1)
     partial_sums = far_terms(own_obs, points, source_re, source_im)
-    spectra = lax.psum(partial_sums, ("flow", "col"))
+    spectra = choose_tails(partial_sums)
     return (state, spectra)
 
 

time: 144 us -> 131 us (0.910)
  blocking collectives: 53.4 us -> 39.4 us
    psum x1 -> x0, blocking collectives: 25.7 us -> none  [on_device(): spectra = lax.psum(partial_sums, ('flow', 'col'))]
    all_gather x0 -> x1, blocking collectives: none -> 11.7 us  [switch_ladders_here(): return jax.lax.all_gather(mat, mesh_ax).sum(axis=0)]
  transfers between devices with their start and end apart: 12 -> 12, of which waited for: 5 -> 5; matrix products, arithmetic and copies ran while one was open for 20% -> 22% of each run, Pallas kernels for 0% -> 0%
where the time goes in v1:
time: 131 us; the launch traced here: 130 us
  blocking collectives  39.4 us (30%)
  starting transfers between devices  30.3 us (23%)
  local copies, waits for them, and re-layouts  19.8 us (15%)
  matrix products  17.4 us (13%)
  waiting for transfers between devices  11.9 us (9%)
  other arithmetic  10.4 us (8%)
  between operations  1.33 us (1%)
    ppermute x6, starting transfers between devices, with_halo(): before = lax.ppermute(last, axis, up)  22.3 us
    all_gather x1, blocking collectives, on_device(): lax.all_gather(surface_samples, 'row', axis=2, tiled=True)  14.4 us
    all_gather x1, blocking collectives, on_device(): lax.all_gather(panel_points, 'row', axis=1, tiled=True)  13.2 us
    all_gather x1, blocking collectives, switch_ladders_here(): return jax.lax.all_gather(mat, mesh_ax).sum(axis=0)  11.7 us
    dot_general x12, matrix products, contract_small(): result = jnp.einsum('...p,qp->...q', blocked, matrix, precision=HIGH)  11.6 us
    ppermute x6, starting transfers between devices, with_halo(): after = lax.ppermute(first, axis, down)  7.92 us
    ppermute x6, waiting for transfers between devices, with_halo(): after = lax.ppermute(first, axis, down)  6.94 us
    mul x1, other arithmetic, on_device(): wide_back = jnp.kron(identity, eigen_bases[2])  4.95 us
  transfers between devices with their start and end apart: 12, of which 5 were waited for; matrix products, arithmetic and copies ran while one was open for 22% of the time, Pallas kernels for 0%

profile of v1, /device:TPU:0, one launch (start us, length us, event | category | flops | bytes accessed | tf_op | source)
XLA Modules:
  0.0 130.4 jit_solution(9131583842818226557)
XLA Ops:
  0.6 0.9 fusion.168
  1.7 1.3 collective-permute-start
  3.0 4.8 %collective-permute-start.1 = (f32[5,1,12,192]{3,1,2,0:T(1,128)S(1)}, f32[5,1,12,192]{3,1,2,0:T(1,128)S(1)}, u32[]{:S(2)}, u32[]{:S(2)}) collective-permute-start(f32[5,1,12,192]{3,1,2,0:T(1,128)S(1)} %copy.139), channel_id=1, source_target_pairs={{0,16},{1,17},{2,18},{3,19},{4,20},{5,21},{6,22},{7,23},{8,24},{9,... | collective-permute-start | bytes 138248 | tf_op jit(solution)/shard_map/ppermute | solution.py:32
  7.9 1.3 copy.153
  9.2 0.7 slice_bitcast_fusion.12
  10.0 0.8 slice_bitcast_fusion.15
  10.8 0.9 fusion.131
  11.7 4.9 %broadcast_multiply_fusion = (f32[32,6,32,6]{3,2,1,0:T(8,128)}, f32[32,6,32,6]{3,2,1,0:T(8,128)}, f32[32,6,32,6]{3,2,1,0:T(8,128)}) fusion(f32[6,6]{1,0:T(8,128)S(1)} %get-tuple-element.42, f32[32,32]{1,0:T(8,128)S(1)} %fusion.118, f32[6,6]{1,0:T(8,128)S(1)} %copy.146, f32[6,6]{1,0:T(8,128)S(1)} %fusion.131), kind=kLoop, calls=%fused_computation | loop fusion | flops 110592 | bytes 446896 | tf_op jit(solution)/shard_map/jit(kron)/mul | solution.py:122
  16.6 3.9 %reshape.302 = f32[192,192,1,1]{1,0,2,3:T(8,128)S(1)} reshape(f32[32,6,32,6]{3,2,1,0:T(8,128)} %get-tuple-element.41) | data formatting | bytes 294912 | tf_op jit(solution)/shard_map/jit(kron)/mul | solution.py:120
  20.6 0.7 convolution_bitcast_fusion.6
  22.9 13.2 %all-gather.1 = f32[4,32,3]{1,2,0:T(4,128)S(1)} all-gather(f32[1,32,3]{1,2,0:T(4,128)S(1)} %bitcast.284), channel_id=1, replica_groups=mesh['flow'=2,'col'=4,'row'=4] {'row'}, dimensions={0}, use_global_device_ids=true | all-gather | bytes 1920 | tf_op jit(solution)/shard_map/all_gather | solution.py:166
  36.4 0.7 broadcast_multiply_fusion.3
  37.2 0.6 slice_bitcast_fusion.2
  37.8 0.7 add_add_fusion
  38.5 1.1 fusion.3
  39.7 1.3 collective-permute-start.2
  41.0 3.0 %collective-permute-start.3 = (f32[5,8,1,192]{3,1,2,0:T(8,128)S(1)}, f32[5,8,1,192]{3,1,2,0:T(8,128)S(1)}, u32[]{:S(2)}, u32[]{:S(2)}) collective-permute-start(f32[5,8,1,192]{3,1,2,0:T(8,128)S(1)} %get-tuple-element.14), channel_id=1, source_target_pairs={{0,4},{4,8},{8,12},{1,5},{5,9},{9,13},{2,6},{6,10},{10,14},{3,7},{... | collective-permute-start | bytes 92168 | tf_op jit(solution)/shard_map/ppermute | solution.py:32
  44.1 0.8 collective-permute-done.3
  45.3 4.2 %collective-permute-start.5 = (f32[5,8,14,1]{3,1,2,0:T(8,128)S(1)}, f32[5,8,14,1]{3,1,2,0:T(8,128)}, u32[]{:S(2)}, u32[]{:S(2)}) collective-permute-start(f32[5,8,14,1]{3,1,2,0:T(8,128)S(1)} %get-tuple-element.19), channel_id=1, source_target_pairs={{0,1},{1,2},{2,3},{4,5},{5,6},{6,7},{8,9},{9,10},{10,11},{12,13},{... | collective-permute-start | bytes 6728 | tf_op jit(solution)/shard_map/ppermute | solution.py:32
  49.5 1.5 %collective-permute-start.4 = (f32[5,8,14,1]{3,1,2,0:T(8,128)S(1)}, f32[5,8,14,1]{3,1,2,0:T(8,128)}, u32[]{:S(2)}, u32[]{:S(2)}) collective-permute-start(f32[5,8,14,1]{3,1,2,0:T(8,128)S(1)} %get-tuple-element.18), channel_id=1, source_target_pairs={{1,0},{2,1},{3,2},{5,4},{6,5},{7,6},{9,8},{10,9},{11,10},{13,12},{... | collective-permute-start | bytes 6728 | tf_op jit(solution)/shard_map/ppermute | solution.py:33
  51.0 3.9 %reshape.305 = f32[192,192,1,1]{1,0,2,3:T(8,128)S(1)} reshape(f32[32,6,32,6]{3,2,1,0:T(8,128)} %get-tuple-element.40) | data formatting | bytes 294912 | tf_op jit(solution)/shard_map/jit(kron)/mul | solution.py:121
  54.8 3.9 %reshape.308 = f32[192,192,1,1]{1,0,2,3:T(8,128)S(1)} reshape(f32[32,6,32,6]{3,2,1,0:T(8,128)} %get-tuple-element.39) | data formatting | bytes 294912 | tf_op jit(solution)/shard_map/jit(kron)/mul | solution.py:122
  58.8 2.2 %collective-permute-done.4 = f32[5,8,14,1]{3,1,2,0:T(8,128)} collective-permute-done((f32[5,8,14,1]{3,1,2,0:T(8,128)S(1)}, f32[5,8,14,1]{3,1,2,0:T(8,128)}, u32[]{:S(2)}, u32[]{:S(2)}) %collective-permute-start.4) | collective-permute-done | bytes 2272 | tf_op jit(solution)/shard_map/ppermute | solution.py:33
  61.0 2.7 %fusion.55 = f32[5,12,192,6]{2,3,1,0:T(8,128)S(1)} fusion(f32[5,6,12,192]{3,1,2,0:T(8,128)S(1)} %fusion.3, f32[5,8,14,1]{3,1,2,0:T(8,128)} %collective-permute-done.5, f32[5,8,1,192]{3,1,2,0:T(8,128)S(1)} %collective-permute-done.2, f32[5,8,1,192]{3,1,2,0:T(8,128)S(1)} %collective-permute-done.3, f32[5,1,12,192]{3,1,2,0:T(1,128)S(1)} %collective-permute-done, ...), kind=kOutput, calls=%fused_computation.96 | convolution fusion | flops 7119360 | bytes 1476992 | tf_op jit(solution)/shard_map/...p,qp->...q/dot_general | solution.py:43
  63.8 0.6 convolution_bitcast_fusion.5
  65.3 0.8 fusion.90
  66.1 0.6 convolution_bitcast_fusion.4
  66.9 0.8 fusion.10
  67.9 1.3 collective-permute-start.6
  69.2 4.5 %collective-permute-start.7 = (f32[5,1,12,192]{3,1,2,0:T(1,128)S(1)}, f32[5,1,12,192]{3,1,2,0:T(1,128)S(1)}, u32[]{:S(2)}, u32[]{:S(2)}) collective-permute-start(f32[5,1,12,192]{3,1,2,0:T(1,128)S(1)} %get-tuple-element.20), channel_id=1, source_target_pairs={{0,16},{1,17},{2,18},{3,19},{4,20},{5,21},{6,22},{7,23},{8,24},{9,... | collective-permute-start | bytes 138248 | tf_op jit(solution)/shard_map/ppermute | solution.py:32
  74.4 1.2 collective-permute-done.7
  75.6 1.3 collective-permute-start.8
  76.9 3.3 %collective-permute-start.9 = (f32[5,8,1,192]{3,1,2,0:T(8,128)S(1)}, f32[5,8,1,192]{3,1,2,0:T(8,128)S(1)}, u32[]{:S(2)}, u32[]{:S(2)}) collective-permute-start(f32[5,8,1,192]{3,1,2,0:T(8,128)S(1)} %get-tuple-element.12), channel_id=1, source_target_pairs={{0,4},{4,8},{8,12},{1,5},{5,9},{9,13},{2,6},{6,10},{10,14},{3,7},{... | collective-permute-start | bytes 92168 | tf_op jit(solution)/shard_map/ppermute | solution.py:32
  80.2 0.6 convolution_bitcast_fusion.2
  81.4 2.4 %collective-permute-start.11 = (f32[5,8,14,1]{3,1,2,0:T(8,128)S(1)}, f32[5,8,14,1]{3,1,2,0:T(8,128)S(1)}, u32[]{:S(2)}, u32[]{:S(2)}) collective-permute-start(f32[5,8,14,1]{3,1,2,0:T(8,128)S(1)} %get-tuple-element.17), channel_id=1, source_target_pairs={{0,1},{1,2},{2,3},{4,5},{5,6},{6,7},{8,9},{9,10},{10,11},{12,13},{... | collective-permute-start | bytes 6728 | tf_op jit(solution)/shard_map/ppermute | solution.py:32
  83.8 1.3 collective-permute-start.10
  85.1 0.8 fusion.7
  85.9 2.9 %collective-permute-done.11 = f32[5,8,14,1]{3,1,2,0:T(8,128)S(1)} collective-permute-done((f32[5,8,14,1]{3,1,2,0:T(8,128)S(1)}, f32[5,8,14,1]{3,1,2,0:T(8,128)S(1)}, u32[]{:S(2)}, u32[]{:S(2)}) %collective-permute-start.11) | collective-permute-done | bytes 2272 | tf_op jit(solution)/shard_map/ppermute | solution.py:32
  88.8 4.7 %collective-permute-done.10 = f32[5,8,14,1]{3,1,2,0:T(8,128)S(1)} collective-permute-done((f32[5,8,14,1]{3,1,2,0:T(8,128)S(1)}, f32[5,8,14,1]{3,1,2,0:T(8,128)S(1)}, u32[]{:S(2)}, u32[]{:S(2)}) %collective-permute-start.10) | collective-permute-done | bytes 2272 | tf_op jit(solution)/shard_map/ppermute | solution.py:33
  93.5 1.7 %fusion.28 = f32[5,12,192,6]{2,3,1,0:T(8,128)S(1)} fusion(f32[5,6,12,192]{3,1,2,0:T(8,128)S(1)} %fusion.7, f32[5,8,14,1]{3,1,2,0:T(8,128)S(1)} %collective-permute-done.11, f32[5,8,1,192]{3,1,2,0:T(8,128)S(1)} %collective-permute-done.8, f32[5,8,1,192]{3,1,2,0:T(8,128)S(1)} %collective-permute-done.9, f32[5,1,12,192]{3,1,2,0:T(1,128)S(1)} %collective-permute-done.6, ...), kind=kOutput, calls=%fused_computation.57 | convolution fusion | flops 7119360 | bytes 2045952 | tf_op jit(solution)/shard_map/...p,qp->...q/dot_general | solution.py:43
  95.2 0.6 convolution_bitcast_fusion.1
  96.7 0.8 fusion.84
  97.5 0.6 convolution_bitcast_fusion
  98.3 0.7 fusion.8
  99.0 0.9 copy.174
  100.2 14.4 %all_gather.13 = f32[4,16,128]{1,0,2:T(4,128)S(1)} all-gather(f32[4,16,32]{1,0,2:T(4,128)S(1)} %pad_maximum_fusion.62), channel_id=1, replica_groups=mesh['flow'=2,'col'=4,'row'=4] {'row'}, dimensions={2}, use_global_device_ids=true | all-gather | bytes 40960 | tf_op jit(solution)/shard_map/all_gather | solution.py:167
  115.4 2.7 %fusion.17 = (f32[16,64]{1,0:T(8,128)S(1)}, f32[16,64]{1,0:T(8,128)S(1)}) fusion(f32[16,128]{1,0:T(8,128)S(1)} %get-tuple-element.36, f32[64,128]{1,0:T(8,128)S(1)} %copy-done.6, f32[64,128]{1,0:T(8,128)S(1)} %copy-done.7, f32[16,128]{1,0:T(8,128)S(1)} %get-tuple-element.37, f32[16,128]{1,0:T(8,128)S(1)} %get-tuple-element.38, ...), kind=kLoop, calls=%fused_computation.41 | loop fusion | flops 3799040 | bytes 303232 | tf_op jit(solution)/shard_map/reduce_sum | solution.py:84
  118.1 11.7 %all-gather = f32[16,16,64]{2,1,0:T(8,128)S(1)} all-gather(f32[2,16,64]{2,1,0:T(8,128)S(1)} %pad_maximum_fusion.69), channel_id=2, replica_groups=mesh['flow'=2,'col'=4,'row'=4] {'flow','col'}, dimensions={0}, use_global_device_ids=true | all-gather | bytes 73728 | tf_op jit(solution)/shard_map/all_gather | solution.py:19
  (87 shorter events, 7.6 us)
Async XLA Ops:
  0.6 35.6 %copy-start = (f32[3,256]{1,0:T(4,128)S(1)}, f32[3,256]{1,0:T(4,128)}, u32[]{:S(2)}) copy-start(f32[3,256]{1,0:T(4,128)} %param.13) | copy-start | bytes 9220
  1.7 38.0 %collective-permute-start = (f32[5,1,12,192]{3,1,2,0:T(1,128)S(1)}, f32[5,1,12,192]{3,1,2,0:T(1,128)S(1)}, u32[]{:S(2)}, u32[]{:S(2)}) collective-permute-start(f32[5,1,12,192]{3,1,2,0:T(1,128)S(1)} %copy.137), channel_id=1, source_target_pairs={{16,0},{17,1},{18,2},{19,3},{20,4},{21,5},{22,6},{23,7},{24,8},{25... | collective-permute-start | bytes 138248 | tf_op jit(solution)/shard_map/ppermute | solution.py:33
  3.0 36.6 %collective-permute-start.1 = (f32[5,1,12,192]{3,1,2,0:T(1,128)S(1)}, f32[5,1,12,192]{3,1,2,0:T(1,128)S(1)}, u32[]{:S(2)}, u32[]{:S(2)}) collective-permute-start(f32[5,1,12,192]{3,1,2,0:T(1,128)S(1)} %copy.139), channel_id=1, source_target_pairs={{0,16},{1,17},{2,18},{3,19},{4,20},{5,21},{6,22},{7,23},{8,24},{9,... | collective-permute-start | bytes 138248 | tf_op jit(solution)/shard_map/ppermute | solution.py:32
  16.6 4.0 %copy-start.1 = (f32[5,6,12,192]{3,2,1,0:T(8,128)S(1)}, f32[5,6,12,192]{3,2,1,0:T(8,128)}, u32[]{:S(2)}) copy-start(f32[5,6,12,192]{3,2,1,0:T(8,128)} %param.9) | copy-start | bytes 829444
  16.6 4.7 %copy-start.3 = (f32[3,6,6]{2,1,0:T(8,128)S(1)}, f32[3,6,6]{2,1,0:T(8,128)}, u32[]{:S(2)}) copy-start(f32[3,6,6]{2,1,0:T(8,128)} %param.11) | copy-start | bytes 1300
  16.6 5.8 %copy-start.13 = (f32[1,2,32]{2,1,0:T(2,128)S(1)}, f32[1,2,32]{2,1,0:T(2,128)}, u32[]{:S(2)}) copy-start(f32[1,2,32]{2,1,0:T(2,128)} %param.10) | copy-start | bytes 772
  16.6 6.3 %copy-start.12 = (f32[3,32]{1,0:T(4,128)S(1)}, f32[3,32]{1,0:T(4,128)}, u32[]{:S(2)}) copy-start(f32[3,32]{1,0:T(4,128)} %param.14) | copy-start | bytes 1156
  16.6 21.9 %copy-start.2 = (f32[5,6,12,192]{3,2,1,0:T(8,128)S(1)}, f32[5,6,12,192]{3,2,1,0:T(8,128)}, u32[]{:S(2)}) copy-start(f32[5,6,12,192]{3,2,1,0:T(8,128)} %param.8) | copy-start | bytes 829444
  39.7 4.4 %collective-permute-start.2 = (f32[5,8,1,192]{3,1,2,0:T(8,128)S(1)}, f32[5,8,1,192]{3,1,2,0:T(8,128)S(1)}, u32[]{:S(2)}, u32[]{:S(2)}) collective-permute-start(f32[5,8,1,192]{3,1,2,0:T(8,128)S(1)} %get-tuple-element.15), channel_id=1, source_target_pairs={{4,0},{8,4},{12,8},{5,1},{9,5},{13,9},{6,2},{10,6},{14,10},{7,3},{... | collective-permute-start | bytes 92168 | tf_op jit(solution)/shard_map/ppermute | solution.py:33
  41.0 3.9 %collective-permute-start.3 = (f32[5,8,1,192]{3,1,2,0:T(8,128)S(1)}, f32[5,8,1,192]{3,1,2,0:T(8,128)S(1)}, u32[]{:S(2)}, u32[]{:S(2)}) collective-permute-start(f32[5,8,1,192]{3,1,2,0:T(8,128)S(1)} %get-tuple-element.14), channel_id=1, source_target_pairs={{0,4},{4,8},{8,12},{1,5},{5,9},{9,13},{2,6},{6,10},{10,14},{3,7},{... | collective-permute-start | bytes 92168 | tf_op jit(solution)/shard_map/ppermute | solution.py:32
  45.3 13.6 %collective-permute-start.5 = (f32[5,8,14,1]{3,1,2,0:T(8,128)S(1)}, f32[5,8,14,1]{3,1,2,0:T(8,128)}, u32[]{:S(2)}, u32[]{:S(2)}) collective-permute-start(f32[5,8,14,1]{3,1,2,0:T(8,128)S(1)} %get-tuple-element.19), channel_id=1, source_target_pairs={{0,1},{1,2},{2,3},{4,5},{5,6},{6,7},{8,9},{9,10},{10,11},{12,13},{... | collective-permute-start | bytes 6728 | tf_op jit(solution)/shard_map/ppermute | solution.py:32
  49.5 11.6 %collective-permute-start.4 = (f32[5,8,14,1]{3,1,2,0:T(8,128)S(1)}, f32[5,8,14,1]{3,1,2,0:T(8,128)}, u32[]{:S(2)}, u32[]{:S(2)}) collective-permute-start(f32[5,8,14,1]{3,1,2,0:T(8,128)S(1)} %get-tuple-element.18), channel_id=1, source_target_pairs={{1,0},{2,1},{3,2},{5,4},{6,5},{7,6},{9,8},{10,9},{11,10},{13,12},{... | collective-permute-start | bytes 6728 | tf_op jit(solution)/shard_map/ppermute | solution.py:33
  51.0 7.7 %copy-start.11 = (f32[4,15,32]{2,0,1:T(4,128)S(1)}, f32[4,15,32]{2,0,1:T(4,128)}, u32[]{:S(2)}) copy-start(f32[4,15,32]{2,0,1:T(4,128)} %param.15) | copy-start | bytes 23044
  61.0 3.6 %copy-start.4 = (f32[6,12,192]{2,1,0:T(8,128)S(1)}, f32[6,12,192]{2,1,0:T(8,128)}, u32[]{:S(2)}) copy-start(f32[6,12,192]{2,1,0:T(8,128)} %add_add_fusion) | copy-start | bytes 165892
  67.9 6.5 %collective-permute-start.6 = (f32[5,1,12,192]{3,1,2,0:T(1,128)S(1)}, f32[5,1,12,192]{3,1,2,0:T(1,128)S(1)}, u32[]{:S(2)}, u32[]{:S(2)}) collective-permute-start(f32[5,1,12,192]{3,1,2,0:T(1,128)S(1)} %get-tuple-element.21), channel_id=1, source_target_pairs={{16,0},{17,1},{18,2},{19,3},{20,4},{21,5},{22,6},{23,7},{24,8},{25... | collective-permute-start | bytes 138248 | tf_op jit(solution)/shard_map/ppermute | solution.py:33
  69.2 6.4 %collective-permute-start.7 = (f32[5,1,12,192]{3,1,2,0:T(1,128)S(1)}, f32[5,1,12,192]{3,1,2,0:T(1,128)S(1)}, u32[]{:S(2)}, u32[]{:S(2)}) collective-permute-start(f32[5,1,12,192]{3,1,2,0:T(1,128)S(1)} %get-tuple-element.20), channel_id=1, source_target_pairs={{0,16},{1,17},{2,18},{3,19},{4,20},{5,21},{6,22},{7,23},{8,24},{9,... | collective-permute-start | bytes 138248 | tf_op jit(solution)/shard_map/ppermute | solution.py:32
  75.6 5.4 %collective-permute-start.8 = (f32[5,8,1,192]{3,1,2,0:T(8,128)S(1)}, f32[5,8,1,192]{3,1,2,0:T(8,128)S(1)}, u32[]{:S(2)}, u32[]{:S(2)}) collective-permute-start(f32[5,8,1,192]{3,1,2,0:T(8,128)S(1)} %get-tuple-element.13), channel_id=1, source_target_pairs={{4,0},{8,4},{12,8},{5,1},{9,5},{13,9},{6,2},{10,6},{14,10},{7,3},{... | collective-permute-start | bytes 92168 | tf_op jit(solution)/shard_map/ppermute | solution.py:33
  76.9 4.1 %collective-permute-start.9 = (f32[5,8,1,192]{3,1,2,0:T(8,128)S(1)}, f32[5,8,1,192]{3,1,2,0:T(8,128)S(1)}, u32[]{:S(2)}, u32[]{:S(2)}) collective-permute-start(f32[5,8,1,192]{3,1,2,0:T(8,128)S(1)} %get-tuple-element.12), channel_id=1, source_target_pairs={{0,4},{4,8},{8,12},{1,5},{5,9},{9,13},{2,6},{6,10},{10,14},{3,7},{... | collective-permute-start | bytes 92168 | tf_op jit(solution)/shard_map/ppermute | solution.py:32
  81.4 7.4 %collective-permute-start.11 = (f32[5,8,14,1]{3,1,2,0:T(8,128)S(1)}, f32[5,8,14,1]{3,1,2,0:T(8,128)S(1)}, u32[]{:S(2)}, u32[]{:S(2)}) collective-permute-start(f32[5,8,14,1]{3,1,2,0:T(8,128)S(1)} %get-tuple-element.17), channel_id=1, source_target_pairs={{0,1},{1,2},{2,3},{4,5},{5,6},{6,7},{8,9},{9,10},{10,11},{12,13},{... | collective-permute-start | bytes 6728 | tf_op jit(solution)/shard_map/ppermute | solution.py:32
  83.8 9.7 %collective-permute-start.10 = (f32[5,8,14,1]{3,1,2,0:T(8,128)S(1)}, f32[5,8,14,1]{3,1,2,0:T(8,128)S(1)}, u32[]{:S(2)}, u32[]{:S(2)}) collective-permute-start(f32[5,8,14,1]{3,1,2,0:T(8,128)S(1)} %get-tuple-element.16), channel_id=1, source_target_pairs={{1,0},{2,1},{3,2},{5,4},{6,5},{7,6},{9,8},{10,9},{11,10},{13,12},{... | collective-permute-start | bytes 6728 | tf_op jit(solution)/shard_map/ppermute | solution.py:33
  97.4 17.9 %copy-start.5 = (f32[64,128]{1,0:T(8,128)S(1)}, f32[64,128]{1,0:T(8,128)}, u32[]{:S(2)}) copy-start(f32[64,128]{1,0:T(8,128)} %get-tuple-element.27) | copy-start | bytes 98308
  97.4 17.9 %copy-start.6 = (f32[64,128]{1,0:T(8,128)S(1)}, f32[64,128]{1,0:T(8,128)}, u32[]{:S(2)}) copy-start(f32[64,128]{1,0:T(8,128)} %get-tuple-element.28) | copy-start | bytes 98308
  97.4 17.9 %copy-start.7 = (f32[64,128]{1,0:T(8,128)S(1)}, f32[64,128]{1,0:T(8,128)}, u32[]{:S(2)}) copy-start(f32[64,128]{1,0:T(8,128)} %get-tuple-element.30) | copy-start | bytes 98308
  97.4 17.9 %copy-start.8 = (f32[64,128]{1,0:T(8,128)S(1)}, f32[64,128]{1,0:T(8,128)}, u32[]{:S(2)}) copy-start(f32[64,128]{1,0:T(8,128)} %get-tuple-element.24) | copy-start | bytes 98308
  97.5 17.9 %copy-start.9 = (f32[64,128]{1,0:T(8,128)S(1)}, f32[64,128]{1,0:T(8,128)}, u32[]{:S(2)}) copy-start(f32[64,128]{1,0:T(8,128)} %get-tuple-element.25) | copy-start | bytes 98308
  97.5 17.9 %copy-start.10 = (f32[64,128]{1,0:T(8,128)S(1)}, f32[64,128]{1,0:T(8,128)}, u32[]{:S(2)}) copy-start(f32[64,128]{1,0:T(8,128)} %get-tuple-element.26) | copy-start | bytes 98308
